TPU v7x, 32 devices: a whole 2x2x4 slice. The times are simulated.
32 devices in a mesh: group: 2 (over x), expert: 8 (over z, y), tensor: 2 (over core).
Axes of the slice: x: 2, y: 2, z: 4, core: 2. Of those that a mesh axis runs over, the one named last changes fastest.
Arguments:
- grad_out: bfloat16 [4096, 4096], P(('group', 'expert', 'tensor')), parts along dimension 0, may hold values from -6 to 6
- expert_ids: int32 [4096, 2], P(('group', 'expert', 'tensor')), parts along dimension 0, may hold values from 0 to 3, all different within a row; in each aligned block of 128 rows (0 to 127, 128 to 255, ...) at most 96 rows name the same one
- probs: float32 [4096, 2], P(('group', 'expert', 'tensor')), parts along dimension 0, may hold values from 0.1 to 1
- saved_gate: bfloat16 [8, 16, 2, 96, 768], P('expert', 'group', None, None, 'tensor'), parts along dimension 1, may hold values from -6 to 6
- saved_up: bfloat16 [8, 16, 2, 96, 768], P('expert', 'group', None, None, 'tensor'), parts along dimension 1, may hold values from -6 to 6
- gate_weight: bfloat16 [8, 4096, 768], P('expert', None, 'tensor'), may hold values from -0.09375 to 0.09375
- up_weight: bfloat16 [8, 4096, 768], P('expert', None, 'tensor'), may hold values from -0.09375 to 0.09375
- down_weight: bfloat16 [8, 768, 4096], P('expert', 'tensor'), may hold values from -0.15625 to 0.15625
Outputs:
- grad_in: bfloat16 [4096, 4096], P(('group', 'expert', 'tensor')), parts along dimension 0
There are 2 independent parts, one for each index of `group`. A program takes and returns all parts, laid end to end along the dimension named above; an argument that names none is the same for every part. Nothing has to cross between parts.
Inputs may be any that keep to these rules, and one draw needn't show every extreme that they name: `expert_ids`: each token names 2 different experts; among the 128 tokens of one device no expert is named more than 96 times, and in every draw some expert is named exactly 96 times by one device's tokens.
All inputs are finite; a program needn't handle non-finite values.
Results may differ from a plain program's by a relative error of at most 0.0065.
Values may be sent and summed in bfloat16 or wider, within the bound.
A program may use at most 128 MiB of HBM per device.

v0:
```python
import jax
import jax.numpy as jnp
from jax import lax
from jax.sharding import PartitionSpec as P

TOPK = 2


def shards(grad_out, expert_ids, probs, saved_gate, saved_up, gate_weight, up_weight, down_weight):
    n_expert = lax.axis_size("expert")
    n_tensor = lax.axis_size("tensor")
    experts = n_expert // 2
    capacity = saved_gate.shape[3]
    tok_rows = grad_out.shape[0]
    width = grad_out.shape[1]
    picks = tok_rows * TOPK
    chosen = expert_ids.reshape(picks)
    onehot = (chosen[:, None] == jnp.arange(experts, dtype=jnp.int32)[None, :]).astype(jnp.int32)
    earlier = jnp.cumsum(onehot, axis=0) - onehot
    position = jnp.sum(earlier * onehot, axis=1)
    target = chosen * capacity + position
    places = jnp.arange(experts * capacity, dtype=jnp.int32)
    placing = (places[:, None] == target[None, :]).astype(jnp.bfloat16)
    repeated = jnp.repeat(grad_out, TOPK, axis=0)
    packed = jnp.dot(placing, repeated, preferred_element_type=jnp.float32).astype(jnp.bfloat16)
    halves = jnp.broadcast_to(
        packed.reshape(experts, 1, capacity, width), (experts, 2, capacity, width)
    )
    outgoing = jnp.broadcast_to(halves[:, :, None], (experts, 2, n_tensor, capacity, width))
    outgoing = outgoing.reshape(n_expert * n_tensor, capacity, width)
    arrived = lax.all_to_all(
        outgoing, ("expert", "tensor"), split_axis=0, concat_axis=0, tiled=True
    )
    arrived = arrived.reshape(n_expert, n_tensor, capacity, width)
    rows = arrived.reshape(n_expert * n_tensor * capacity, width)
    quarter = down_weight.shape[1]
    grad_hidden = lax.dot_general(
        rows, down_weight[0], (((1,), (1,)), ((), ())), preferred_element_type=jnp.float32
    )
    gate_pre = saved_gate[0].reshape(-1, quarter).astype(jnp.float32)
    up_pre = saved_up[0].reshape(-1, quarter).astype(jnp.float32)
    logistic = jax.nn.sigmoid(gate_pre)
    grad_gate = (grad_hidden * up_pre * logistic * (1.0 + gate_pre * (1.0 - logistic))).astype(
        jnp.bfloat16
    )
    grad_up = (grad_hidden * gate_pre * logistic).astype(jnp.bfloat16)
    partial_in = lax.dot_general(
        grad_gate, gate_weight[0], (((1,), (1,)), ((), ())), preferred_element_type=jnp.float32
    )
    partial_in = partial_in + lax.dot_general(
        grad_up, up_weight[0], (((1,), (1,)), ((), ())), preferred_element_type=jnp.float32
    )
    summed = lax.psum_scatter(
        partial_in.reshape(n_expert, n_tensor, capacity, width).astype(jnp.bfloat16),
        "tensor",
        scatter_dimension=1,
        tiled=True,
    )
    backward = summed.reshape(n_expert, capacity, width)
    returned = lax.all_to_all(backward, "expert", split_axis=0, concat_axis=0, tiled=True)
    pair = jnp.sum(returned.reshape(experts, 2, capacity, width).astype(jnp.float32), axis=1)
    pair = pair.reshape(experts * capacity, width)
    matches = (target.reshape(tok_rows, TOPK)[:, :, None] == places[None, None, :]).astype(
        jnp.float32
    )
    combine = jnp.sum(matches * probs[:, :, None], axis=1)
    grad_in = jnp.dot(
        combine, pair, precision=lax.Precision.HIGHEST, preferred_element_type=jnp.float32
    )
    return grad_in.astype(jnp.bfloat16)


def solution(mesh):
    in_specs = (
        P(("group", "expert", "tensor"), None),
        P(("group", "expert", "tensor"), None),
        P(("group", "expert", "tensor"), None),
        P("expert", "group", None, None, "tensor"),
        P("expert", "group", None, None, "tensor"),
        P("expert", None, "tensor"),
        P("expert", None, "tensor"),
        P("expert", "tensor", None),
    )
    out_specs = P(("group", "expert", "tensor"), None)
    return jax.shard_map(shards, mesh=mesh, in_specs=in_specs, out_specs=out_specs, check_vma=False)
```

profile of v0, /device:TPU:8, one launch (start us, length us, event | category | flops | bytes accessed | tf_op | source)
XLA Modules:
  0.0 564.0 jit_solution(14443243862782921958)
XLA Ops:
  6.5 0.0 copy-start
  6.5 0.0 all-reduce.3.cloned.1.call-start
  6.5 0.9 copy.34
  7.5 0.1 eq.55
  7.6 0.1 eq.51
  7.8 1.2 reduce-window.6
  9.0 0.1 slice.8
  9.1 0.1 copy.36
  9.2 0.1 copy.37
  9.3 0.1 add_bitcast_fusion
  9.4 4.6 broadcast_in_dim.2
  14.0 4.1 reshape.60
  18.1 4.3 convolution_convert_fusion
  22.4 8.1 %broadcast_in_dim_broadcast_in_dim_broadcast_in_dim.2 = bf16[4,2,2,96,4096]{4,3,2,1,0:T(8,128)(2,1)} broadcast(bf16[4,96,4096]{2,1,0:T(8,128)(2,1)} %bitcast.56), dimensions={0,3,4} | broadcast | bytes 15728640 | tf_op jit(solution)/shard_map/broadcast_in_dim;broadcast_in_dim;broadcast_in_dim | solution.py:29
  30.5 0.0 copy-start.6
  30.5 278.6 %all_to_all.10 = bf16[16,96,4096]{2,1,0:T(8,128)(2,1)S(1)} all-to-all(bf16[16,96,4096]{2,1,0:T(8,128)(2,1)} %bitcast.54), channel_id=1, replica_groups=mesh['group'=2,'expert'=8,'tensor'=2] {'expert','tensor'}, dimensions={0} | all-to-all | bytes 25165824 | tf_op jit(solution)/shard_map/all_to_all | solution.py:31
  309.1 0.0 copy-done.6
  309.1 0.0 copy-start.3
  309.1 6.9 %fusion.3 = f32[1536,384]{1,0:T(8,128)S(1)} fusion(bf16[1536,4096]{1,0:T(8,128)(2,1)S(1)} %bitcast.57, bf16[1,384,4096]{2,1,0:T(8,128)(2,1)S(1)} %copy-done.6), kind=kOutput, calls=%fused_computation.11 | convolution fusion | flops 4831838208 | bytes 18087936 | tf_op jit(solution)/shard_map/dot_general | solution.py:37
  316.0 0.0 copy-start.2
  316.0 1.4 copy-done.2
  317.4 0.0 copy-done
  317.4 0.0 copy-done.3
  317.4 13.4 %fusion.1 = f32[1536,4096]{1,0:T(8,128)} fusion(bf16[1,4096,384]{2,1,0:T(8,128)(2,1)S(1)} %copy-done, bf16[1536,384]{1,0:T(8,128)(2,1)S(1)} %bitcast.59, f32[1536,384]{1,0:T(8,128)S(1)} %fusion.3, bf16[1536,384]{1,0:T(8,128)(2,1)} %bitcast.60), kind=kOutput, calls=%fused_computation.9 | convolution fusion | flops 4838916096 | bytes 33030144 | tf_op jit(solution)/shard_map/dot_general | solution.py:47
  330.8 16.3 %add_convert_fusion = bf16[1536,4096]{1,0:T(8,128)(2,1)} fusion(f32[1536,4096]{1,0:T(8,128)} %fusion.1, bf16[1,4096,384]{2,1,0:T(8,128)(2,1)} %param.14, f32[1536,384]{1,0:T(8,128)} %copy-done.2, bf16[1536,384]{1,0:T(8,128)(2,1)} %bitcast.58), kind=kOutput, calls=%fused_computation | convolution fusion | flops 4848549888 | bytes 44433408 | tf_op jit(solution)/shard_map/dot_general | solution.py:50
  347.1 0.0 copy-start.7
  347.1 0.0 all-reduce.3.cloned.1.call-update
  347.1 0.6 copy-done.7
  347.7 0.6 dynamic-slice
  348.3 49.6 %all-reduce.3.cloned.1.call-done = bf16[8,2,96,4096]{3,2,1,0:T(8,128)(2,1)} async-done(((bf16[8,2,96,4096]{3,2,1,0:T(8,128)(2,1)}), bf16[8,2,96,4096]{3,2,1,0:T(8,128)(2,1)}) %all-reduce.3.cloned.1.call-update) | async-done | bytes 12582928
  397.9 6.8 %dynamic-slice_bitcast_fusion = bf16[8,96,4096]{2,1,0:T(8,128)(2,1)} fusion(bf16[8,2,96,4096]{3,2,1,0:T(8,128)(2,1)} %all-reduce.3.cloned.1.call-done, u32[]{:T(128)} %bitcast.22), kind=kLoop, calls=%fused_computation.2 | loop fusion | bytes 12582916 | tf_op jit(solution)/shard_map/reshape | solution.py:59
  404.8 0.0 copy-start.4
  404.8 0.0 copy-start.5
  404.8 6.2 %all-to-all-start.1 = ((bf16[8,96,4096]{2,1,0:T(8,128)(2,1)}), bf16[8,96,4096]{2,1,0:T(8,128)(2,1)}, u32[]{:S(2)}, u32[]{:S(2)}) async-start(bf16[8,96,4096]{2,1,0:T(8,128)(2,1)} %dynamic-slice_bitcast_fusion), calls=%async_computation.1 | async-start | bytes 12582912 | tf_op jit(solution)/shard_map/all_to_all | solution.py:60
  411.0 0.1 reduce_sum.30
  411.1 0.1 copy.38
  411.2 0.0 copy-done.4
  411.2 0.0 copy-done.5
  411.2 0.1 select_reduce_fusion
  411.3 135.8 %all-to-all-done.1 = bf16[8,96,4096]{2,1,0:T(8,128)(2,1)} async-done(((bf16[8,96,4096]{2,1,0:T(8,128)(2,1)}), bf16[8,96,4096]{2,1,0:T(8,128)(2,1)}, u32[]{:S(2)}, u32[]{:S(2)}) %all-to-all-start.1) | async-done | bytes 6291488 | tf_op jit(solution)/shard_map/all_to_all | solution.py:60
  547.1 5.2 convert_reduce_fusion
  552.3 0.0 copy-start.1
  552.3 4.8 convolution_convert_fusion.1
  557.1 0.0 copy-done.1
  (6 shorter events, 0.1 us)
Async XLA Ops:
  6.5 310.8 %copy-start = (bf16[1,4096,384]{2,1,0:T(8,128)(2,1)S(1)}, bf16[1,4096,384]{2,1,0:T(8,128)(2,1)}, u32[]{:S(2)}) copy-start(bf16[1,4096,384]{2,1,0:T(8,128)(2,1)} %param.13) | copy-start | bytes 9437188
  6.5 391.4 %all-reduce.3.cloned.1.call-start = ((), (), s32[]{:S(2)}) async-start(), calls=%async_computation.2 | async-start | bytes 25165824
  30.5 278.6 %copy-start.6 = (bf16[1,384,4096]{2,1,0:T(8,128)(2,1)S(1)}, bf16[1,384,4096]{2,1,0:T(8,128)(2,1)}, u32[]{:S(2)}) copy-start(bf16[1,384,4096]{2,1,0:T(8,128)(2,1)} %param.15) | copy-start | bytes 9437188
  309.1 8.3 %copy-start.3 = (bf16[1,8,2,96,384]{4,3,2,1,0:T(8,128)(2,1)S(1)}, bf16[1,8,2,96,384]{4,3,2,1,0:T(8,128)(2,1)}, u32[]{:S(2)}) copy-start(bf16[1,8,2,96,384]{4,3,2,1,0:T(8,128)(2,1)} %param.11) | copy-start | bytes 3538948
  316.0 1.4 copy-start.2
  347.1 0.7 copy-start.7
  404.8 6.4 %copy-start.4 = (s32[128,2]{0,1:T(2,128)S(1)}, s32[128,2]{0,1:T(2,128)}, u32[]{:S(2)}) copy-start(s32[128,2]{0,1:T(2,128)} %param.9) | copy-start | bytes 3076
  404.8 6.4 %copy-start.5 = (f32[128,2]{0,1:T(2,128)S(1)}, f32[128,2]{0,1:T(2,128)}, u32[]{:S(2)}) copy-start(f32[128,2]{0,1:T(2,128)} %param.10) | copy-start | bytes 3076
  404.8 142.3 %all-to-all-start.1 = ((bf16[8,96,4096]{2,1,0:T(8,128)(2,1)}), bf16[8,96,4096]{2,1,0:T(8,128)(2,1)}, u32[]{:S(2)}, u32[]{:S(2)}) async-start(bf16[8,96,4096]{2,1,0:T(8,128)(2,1)} %dynamic-slice_bitcast_fusion), calls=%async_computation.1 | async-start | bytes 12582912 | tf_op jit(solution)/shard_map/all_to_all | solution.py:60
  552.3 4.9 copy-start.1
Sparse Core Ops, SparseCore 0:
  347.2 50.6 all-reduce.2
where the time goes:
time: 568 us; the launch traced here: 564 us
  blocking collectives  279 us (49%)
  waiting for transfers between devices  185 us (33%)
  matrix products  45.7 us (8%)
  local copies, waits for them, and re-layouts  28 us (5%)
  between operations  13.5 us (2%)
  other arithmetic  6.68 us (1%)
  starting transfers between devices  6.19 us (1%)
    all_to_all x1, blocking collectives, shards(): lax.all_to_all(outgoing, ('expert', 'tensor'), split_axis=0, concat_axis=...  279 us
    all_to_all x1, waiting for transfers between devices, shards(): lax.all_to_all(backward, 'expert', split_axis=0, concat_axis=0, tiled=True)  136 us
    unnamed x2, waiting for transfers between devices  49.6 us
    dot_general x1, matrix products, shards(): lax.dot_general(grad_up, up_weight[0], (((1,), (1,)), ((), ())), preferre...  16.3 us
    dot_general x1, matrix products, shards(): lax.dot_general(grad_gate, gate_weight[0], (((1,), (1,)), ((), ())), pref...  13.4 us
  transfers between devices with their start and end apart: 2, of which 2 were waited for; matrix products, arithmetic and copies ran while one was open for 0% of the time, Pallas kernels for 0%

commit v1 on v0

v1 whole, which is shorter than its diff:
```python
import functools

import jax
import jax.numpy as jnp
from jax import lax
from jax.experimental import pallas as pl
from jax.experimental.pallas import tpu as pltpu
from jax.sharding import PartitionSpec as P

MESH = pl.DeviceIdType.MESH
F32 = jnp.float32
BF16 = jnp.bfloat16
NT = (((1,), (1,)), ((), ()))


def kernel(
    experts, cap, go_ref, ids_ref, probs_ref, sg_in, su_in, gw_in, uw_in, dw_in, out_ref,
    rows, packed, dw, gw, uw, sg, su, psend, own, precv, ret, acc, key_ref, hid_g, hid_u,
    local_sem, core_send, core_recv, z_send, z_recv, f_send, f_recv, r_send, r_recv, b_send, b_recv,
):
    tok, width = go_ref.shape
    quarter = dw_in.shape[1]
    ff = 2 * quarter
    e = lax.axis_index("expert")
    c = lax.axis_index("tensor")
    x = e // 2
    h = lax.rem(e, 2)
    sibling = {"tensor": 1 - c}
    partner = {"expert": e + 1 - 2 * h}

    def ahead(k):
        return lax.rem(x + k, experts)

    def behind(k):
        return lax.rem(x + experts - k, experts)

    barrier = pltpu.get_barrier_semaphore()
    pl.semaphore_signal(barrier, inc=1, device_id=sibling, device_id_type=MESH)
    pl.semaphore_signal(barrier, inc=1, device_id=partner, device_id_type=MESH)
    for k in range(1, experts):
        pl.semaphore_signal(barrier, inc=1, device_id={"expert": 2 * ahead(k) + h}, device_id_type=MESH)

    lane = lax.broadcasted_iota(jnp.int32, (tok, 128), 1)
    ids = ids_ref[...]
    probs = probs_ref[...]
    named = ((ids[:, 0:1] == lane) | (ids[:, 1:2] == lane)).astype(F32)
    row_i = lax.broadcasted_iota(jnp.int32, (tok, tok), 0)
    col_i = lax.broadcasted_iota(jnp.int32, (tok, tok), 1)
    lower = (col_i < row_i).astype(BF16)
    place = jnp.dot(lower, named.astype(BF16), preferred_element_type=F32)
    key = jnp.where(named > 0.5, place, -1.0)
    key_ref[...] = key
    key_t = key.T
    row_e = lax.broadcasted_iota(jnp.int32, (128, tok), 0)
    slot_r = lax.broadcasted_iota(jnp.int32, (cap, tok), 0).astype(F32)

    chunk = 512
    chunks = width // chunk

    def pack(k, dst):
        line = jnp.sum(jnp.where(row_e == ahead(k), key_t, 0.0), axis=0, keepdims=True)
        select = (line == slot_r).astype(BF16)

        def step(j, carry):
            at = pl.ds(pl.multiple_of(j * chunk, chunk), chunk)
            dst[:, at] = jnp.dot(select, go_ref[:, at], preferred_element_type=F32).astype(BF16)
            return carry

        lax.fori_loop(0, chunks, step, 0)

    def z_copy(k):
        return pltpu.make_async_remote_copy(
            src_ref=packed.at[k - 1], dst_ref=rows.at[k, 0],
            send_sem=z_send.at[k], recv_sem=z_recv.at[k],
            device_id={"expert": 2 * ahead(k) + h}, device_id_type=MESH,
        )

    def f_copy(k):
        return pltpu.make_async_remote_copy(
            src_ref=rows.at[k, 0], dst_ref=rows.at[k, 1],
            send_sem=f_send.at[k], recv_sem=f_recv.at[k],
            device_id=partner, device_id_type=MESH,
        )

    def r_copy(k):
        return pltpu.make_async_remote_copy(
            src_ref=psend.at[k], dst_ref=precv.at[k],
            send_sem=r_send.at[k], recv_sem=r_recv.at[k],
            device_id=partner, device_id_type=MESH,
        )

    def b_copy(k):
        return pltpu.make_async_remote_copy(
            src_ref=rows.at[k, 0], dst_ref=ret.at[k],
            send_sem=b_send.at[k], recv_sem=b_recv.at[k],
            device_id={"expert": 2 * behind(k) + h}, device_id_type=MESH,
        )

    mine = pl.ds(pl.multiple_of(c * quarter, quarter), quarter)
    moves = [
        (dw_in.at[0], dw_in.at[0], dw.at[mine, :]),
        (sg_in.at[0, :, c], sg_in.at[0, :, 1 - c], sg.at[:, :, mine]),
        (su_in.at[0, :, c], su_in.at[0, :, 1 - c], su.at[:, :, mine]),
        (gw_in.at[0], gw_in.at[0], gw.at[:, mine]),
        (uw_in.at[0], uw_in.at[0], uw.at[:, mine]),
    ]
    here = [
        pltpu.make_async_copy(src, dst, local_sem.at[i]) for i, (src, _, dst) in enumerate(moves)
    ]
    across = [
        pltpu.make_async_remote_copy(
            src_ref=src, dst_ref=dst, send_sem=core_send.at[i], recv_sem=core_recv.at[i],
            device_id=sibling, device_id_type=MESH,
        )
        for i, (_, src, dst) in enumerate(moves)
    ]
    order = [0] + sorted(range(1, experts), key=lambda k: -min(k, experts - k))

    pack(order[1], packed.at[order[1] - 1])
    pl.semaphore_wait(barrier, experts + 1)
    z_copy(order[1]).start()
    pack(0, rows.at[0, 0])
    f_copy(0).start()
    for k in order[2:]:
        pack(k, packed.at[k - 1])
        z_copy(k).start()
    for a, b in zip(here, across):
        a.start()
        b.start()

    def forward(k):
        z_copy(k).wait_recv()
        f_copy(k).start()

    hid_step = 256 if ff % 256 == 0 else 128

    def compute(k):
        f_copy(k).wait_recv()
        mine_rows = 2 * behind(k) + h
        other_rows = 2 * behind(k) + 1 - h

        def hidden(j, carry):
            at = pl.ds(pl.multiple_of(j * hid_step, hid_step), hid_step)
            block = rows[k].reshape(2 * cap, width)
            grad = lax.dot_general(block, dw[at, :], NT, preferred_element_type=F32)
            for side, source in enumerate((mine_rows, other_rows)):
                part = grad[side * cap:(side + 1) * cap]
                g = sg[source, :, at].astype(F32)
                u = su[source, :, at].astype(F32)
                sigma = 1.0 / (1.0 + jnp.exp(-g))
                there = pl.ds(side * cap, cap)
                hid_g[there, at] = (part * u * sigma * (1.0 + g * (1.0 - sigma))).astype(BF16)
                hid_u[there, at] = (part * g * sigma).astype(BF16)
            return carry

        lax.fori_loop(0, ff // hid_step, hidden, 0)

        def term(j, carry):
            at = pl.ds(pl.multiple_of(j * chunk, chunk), chunk)
            total = lax.dot_general(hid_g[...], gw[at, :], NT, preferred_element_type=F32)
            total = total + lax.dot_general(hid_u[...], uw[at, :], NT, preferred_element_type=F32)
            own[k, :, at] = total[:cap].astype(own.dtype)
            psend[k, :, at] = total[cap:].astype(BF16)
            return carry

        lax.fori_loop(0, chunks, term, 0)
        r_copy(k).start()

    def settle(k):
        r_copy(k).wait_recv()
        f_copy(k).wait_send()
        dst = ret.at[0] if k == 0 else rows.at[k, 0]

        def step(j, carry):
            at = pl.ds(pl.multiple_of(j * chunk, chunk), chunk)
            dst[:, at] = (own[k, :, at].astype(F32) + precv[k, :, at].astype(F32)).astype(BF16)
            return carry

        lax.fori_loop(0, chunks, step, 0)
        if k != 0:
            b_copy(k).start()

    slot_c = lax.broadcasted_iota(jnp.int32, (tok, cap), 1).astype(F32)

    def combine(k, first, last):
        if k != 0:
            b_copy(k).wait_recv()
        own_x = ahead(k)
        column = jnp.sum(jnp.where(lane == own_x, key_ref[...], 0.0), axis=1, keepdims=True)
        select = (column == slot_c).astype(BF16)
        weight = jnp.sum(jnp.where(ids == own_x, probs, 0.0), axis=1, keepdims=True)

        def step(j, carry):
            at = pl.ds(pl.multiple_of(j * chunk, chunk), chunk)
            value = weight * jnp.dot(select, ret[k, :, at], preferred_element_type=F32)
            if not first:
                value = value + acc[:, at]
            if last:
                out_ref[:, at] = value.astype(BF16)
            else:
                acc[:, at] = value
            return carry

        lax.fori_loop(0, chunks, step, 0)

    for a, b in zip(here, across):
        a.wait()
        b.wait_recv()
    compute(0)
    forward(order[1])
    for i in range(1, experts):
        if i + 1 < experts:
            forward(order[i + 1])
        compute(order[i])
        settle(order[i - 1])
    settle(order[-1])
    for i, k in enumerate(order):
        combine(k, i == 0, i == experts - 1)
    for b in across:
        b.wait_send()
    for k in range(experts):
        r_copy(k).wait_send()
        if k:
            z_copy(k).wait_send()
            b_copy(k).wait_send()


def shards(grad_out, expert_ids, probs, saved_gate, saved_up, gate_weight, up_weight, down_weight):
    n_expert = lax.axis_size("expert")
    experts = n_expert // 2
    tok, width = grad_out.shape
    capacity = saved_gate.shape[3]
    quarter = down_weight.shape[1]
    ff = 2 * quarter
    cap = -(-capacity // 16) * 16
    if cap != capacity:
        pad = ((0, 0), (0, 0), (0, 0), (0, cap - capacity), (0, 0))
        saved_gate = jnp.pad(saved_gate, pad)
        saved_up = jnp.pad(saved_up, pad)
    vmem = pl.BlockSpec(memory_space=pltpu.VMEM)
    hbm = pl.BlockSpec(memory_space=pl.ANY)
    dma = pltpu.SemaphoreType.DMA
    return pl.pallas_call(
        functools.partial(kernel, experts, cap),
        out_shape=jax.ShapeDtypeStruct((tok, width), BF16),
        in_specs=[vmem, vmem, vmem, hbm, hbm, hbm, hbm, hbm],
        out_specs=vmem,
        scratch_shapes=[
            pltpu.VMEM((experts, 2, cap, width), BF16),
            pltpu.VMEM((experts - 1, cap, width), BF16),
            pltpu.VMEM((ff, width), BF16),
            pltpu.VMEM((width, ff), BF16),
            pltpu.VMEM((width, ff), BF16),
            pltpu.VMEM((n_expert, cap, ff), BF16),
            pltpu.VMEM((n_expert, cap, ff), BF16),
            pltpu.VMEM((experts, cap, width), BF16),
            pltpu.VMEM((experts, cap, width), BF16),
            pltpu.VMEM((experts, cap, width), BF16),
            pltpu.VMEM((experts, cap, width), BF16),
            pltpu.VMEM((tok, width), F32),
            pltpu.VMEM((tok, 128), F32),
            pltpu.VMEM((2 * cap, ff), BF16),
            pltpu.VMEM((2 * cap, ff), BF16),
            dma((5,)), dma((5,)), dma((5,)),
            dma((experts,)), dma((experts,)), dma((experts,)), dma((experts,)),
            dma((experts,)), dma((experts,)), dma((experts,)), dma((experts,)),
        ],
        compiler_params=pltpu.CompilerParams(
            collective_id=0, has_side_effects=True, vmem_limit_bytes=63 * 1024 * 1024
        ),
        cost_estimate=pl.CostEstimate(
            flops=6 * n_expert * cap * ff * width, bytes_accessed=8 * width * ff, transcendentals=0
        ),
    )(grad_out, expert_ids, probs, saved_gate, saved_up, gate_weight, up_weight, down_weight)


def solution(mesh):
    in_specs = (
        P(("group", "expert", "tensor"), None),
        P(("group", "expert", "tensor"), None),
        P(("group", "expert", "tensor"), None),
        P("expert", "group", None, None, "tensor"),
        P("expert", "group", None, None, "tensor"),
        P("expert", None, "tensor"),
        P("expert", None, "tensor"),
        P("expert", "tensor", None),
    )
    out_specs = P(("group", "expert", "tensor"), None)
    return jax.shard_map(shards, mesh=mesh, in_specs=in_specs, out_specs=out_specs, check_vma=False)
```

time: 568 us -> 186 us (0.33)
  blocking collectives: 279 us -> 0 us
  waiting for transfers between devices: 185 us -> 0 us
  Pallas kernels: 0 us -> 180 us
  matrix products: 45.7 us -> 0 us
  local copies, waits for them, and re-layouts: 28 us -> 5.1 us
  between operations: 13.5 us -> 0.01 us
  other arithmetic: 6.68 us -> 0 us
  starting transfers between devices: 6.19 us -> 0 us
    all_to_all x1 -> x0, blocking collectives: 279 us -> none  [shards(): lax.all_to_all(outgoing, ('expert', 'tensor'), split_axis=0, concat_axis=...]
    pallas_call x0 -> x1, Pallas kernels: none -> 180 us  [shards(): pl.pallas_call(functools.partial(kernel, experts, cap), out_shape=jax.Sha...]
    all_to_all x1 -> x0, waiting for transfers between devices: 136 us -> none  [shards(): lax.all_to_all(backward, 'expert', split_axis=0, concat_axis=0, tiled=True)]
    unnamed x2 -> x0, waiting for transfers between devices: 49.6 us -> none
    dot_general x5 -> x0, matrix products: 45.7 us -> none  [the longest x1 16.3 us: shards(): lax.dot_general(grad_up, up_weight[0], (((1,), (1,)), ((), ())), preferre...]
    reshape x2 -> x0, local copies, waits for them, and re-layouts: 11 us -> none  [the longest x1 6.84 us: shards(): backward = summed.reshape(n_expert, capacity, width)]
    another operation x3 -> x0, local copies, waits for them, and re-layouts: 8.16 us -> none  [the longest x1 8.06 us: shards(): jnp.broadcast_to(halves[:, :, None], (experts, 2, n_tensor, capacity, wid...]
    all_to_all x1 -> x0, starting transfers between devices: 6.18 us -> none  [shards(): lax.all_to_all(backward, 'expert', split_axis=0, concat_axis=0, tiled=True)]
  transfers between devices with their start and end apart: 2 -> 0, of which waited for: 2 -> 0; matrix products, arithmetic and copies ran while one was open for 0% -> 0% of each run, Pallas kernels for 0% -> 0%
where the time goes in v1:
time: 186 us; the launch traced here: 185 us
  Pallas kernels  180 us (97%)
  local copies, waits for them, and re-layouts  5.1 us (3%)
    pallas_call x1, Pallas kernels, shards(): pl.pallas_call(functools.partial(kernel, experts, cap), out_shape=jax.Sha...  180 us
    unnamed x3, local copies, waits for them, and re-layouts  5.1 us

profile of v1, /device:TPU:8, one launch (start us, length us, event | category | flops | bytes accessed | tf_op | source)
XLA Modules:
  0.0 185.4 jit_solution(6053027423924075371)
XLA Ops:
  0.0 1.4 copy.9.ids_ref
  1.4 1.4 copy.10.probs_ref
  2.8 180.3 %shard_map.82 = bf16[128,4096]{1,0:T(8,128)(2,1)} custom-call(bf16[128,4096]{1,0:T(8,128)(2,1)} %go_ref.1, s32[128,2]{1,0:T(8,128)} %copy.9.ids_ref, f32[128,2]{1,0:T(8,128)} %copy.10.probs_ref, bf16[1,8,2,96,384]{4,3,2,1,0:T(8,128)(2,1)} %sg_in.1, bf16[1,8,2,96,384]{4,3,2,1,0:T(8,128)(2,1)} %su_in.1, bf16[1,4096,384]{2,1,0:T(8,128)(2,1)} %gw_in.1, ...), custom_call_target="tpu_custom_call" | custom-call | flops 14495514624 | bytes 25165824 | tf_op jit(solution)/shard_map/pallas_call | solution.py:243
  183.1 2.3 %copy.12 = bf16[128,4096]{1,0:T(8,128)(2,1)} copy(bf16[128,4096]{1,0:T(8,128)(2,1)} %shard_map.82) | data formatting | bytes 2097152

commit v2 on v1

v2 whole, which is shorter than its diff:
```python
import functools

import jax
import jax.numpy as jnp
from jax import lax
from jax.experimental import pallas as pl
from jax.experimental.pallas import tpu as pltpu
from jax.sharding import PartitionSpec as P

MESH = pl.DeviceIdType.MESH
F32 = jnp.float32
BF16 = jnp.bfloat16
NT = (((1,), (1,)), ((), ()))


def kernel(
    experts, parts, part, go_ref, ids_ref, probs_ref, sg_in, su_in, gw_in, uw_in, dw_in, out_ref,
    rows, packed, dw, gw, uw, sg, su, psend, own, precv, ret, acc, key_ref, hid_g, hid_u,
    local_sem, core_send, core_recv, z_send, z_recv, f_send, f_recv, r_send, r_recv, b_send, b_recv,
):
    tok, width = go_ref.shape
    quarter = dw_in.shape[1]
    ff = 2 * quarter
    e = lax.axis_index("expert")
    c = lax.axis_index("tensor")
    x = e // 2
    h = lax.rem(e, 2)
    sibling = {"tensor": 1 - c}
    partner = {"expert": e + 1 - 2 * h}

    def ahead(k):
        return lax.rem(x + k, experts)

    def behind(k):
        return lax.rem(x + experts - k, experts)

    barrier = pltpu.get_barrier_semaphore()
    pl.semaphore_signal(barrier, inc=1, device_id=sibling, device_id_type=MESH)
    pl.semaphore_signal(barrier, inc=1, device_id=partner, device_id_type=MESH)
    for k in range(1, experts):
        pl.semaphore_signal(barrier, inc=1, device_id={"expert": 2 * ahead(k) + h}, device_id_type=MESH)

    lane = lax.broadcasted_iota(jnp.int32, (tok, 128), 1)
    ids = ids_ref[...]
    probs = probs_ref[...]
    named = ((ids[:, 0:1] == lane) | (ids[:, 1:2] == lane)).astype(F32)
    row_i = lax.broadcasted_iota(jnp.int32, (tok, tok), 0)
    col_i = lax.broadcasted_iota(jnp.int32, (tok, tok), 1)
    lower = (col_i < row_i).astype(BF16)
    place = jnp.dot(lower, named.astype(BF16), preferred_element_type=F32)
    key = jnp.where(named > 0.5, place, -1.0)
    key_ref[...] = key
    key_t = key.T
    row_e = lax.broadcasted_iota(jnp.int32, (128, tok), 0)
    slot_r = lax.broadcasted_iota(jnp.int32, (part, tok), 0)
    lines = [
        jnp.sum(jnp.where(row_e == ahead(k), key_t, 0.0), axis=0, keepdims=True)
        for k in range(experts)
    ]

    chunk = 512
    chunks = width // chunk

    def pack(i):
        slots = (slot_r + i * part).astype(F32)
        select = jnp.concatenate([line == slots for line in lines], axis=0).astype(BF16)

        def step(j, carry):
            at = pl.ds(pl.multiple_of(j * chunk, chunk), chunk)
            got = jnp.dot(select, go_ref[:, at], preferred_element_type=F32).astype(BF16)
            rows[i, 0, 0, :, at] = got[:part]
            for k in range(1, experts):
                packed[i, k - 1, :, at] = got[k * part:(k + 1) * part]
            return carry

        lax.fori_loop(0, chunks, step, 0)

    def z_copy(i, k):
        return pltpu.make_async_remote_copy(
            src_ref=packed.at[i, k - 1], dst_ref=rows.at[i, 0, k],
            send_sem=z_send.at[i, k], recv_sem=z_recv.at[i, k],
            device_id={"expert": 2 * ahead(k) + h}, device_id_type=MESH,
        )

    def f_copy(i, k):
        return pltpu.make_async_remote_copy(
            src_ref=rows.at[i, 0, k], dst_ref=rows.at[i, 1, k],
            send_sem=f_send.at[i, k], recv_sem=f_recv.at[i, k],
            device_id=partner, device_id_type=MESH,
        )

    def r_copy(i, k):
        return pltpu.make_async_remote_copy(
            src_ref=psend.at[i, k], dst_ref=precv.at[i, k],
            send_sem=r_send.at[i, k], recv_sem=r_recv.at[i, k],
            device_id=partner, device_id_type=MESH,
        )

    def b_copy(i, k):
        return pltpu.make_async_remote_copy(
            src_ref=rows.at[i, 0, k], dst_ref=ret.at[i, k],
            send_sem=b_send.at[i, k], recv_sem=b_recv.at[i, k],
            device_id={"expert": 2 * behind(k) + h}, device_id_type=MESH,
        )

    mine = pl.ds(pl.multiple_of(c * quarter, quarter), quarter)
    moves = [
        (dw_in.at[0], dw_in.at[0], dw.at[mine, :]),
        (sg_in.at[0, :, c], sg_in.at[0, :, 1 - c], sg.at[:, :, mine]),
        (su_in.at[0, :, c], su_in.at[0, :, 1 - c], su.at[:, :, mine]),
        (gw_in.at[0], gw_in.at[0], gw.at[:, mine]),
        (uw_in.at[0], uw_in.at[0], uw.at[:, mine]),
    ]
    here = [
        pltpu.make_async_copy(src, dst, local_sem.at[i]) for i, (src, _, dst) in enumerate(moves)
    ]
    across = [
        pltpu.make_async_remote_copy(
            src_ref=src, dst_ref=dst, send_sem=core_send.at[i], recv_sem=core_recv.at[i],
            device_id=sibling, device_id_type=MESH,
        )
        for i, (_, src, dst) in enumerate(moves)
    ]
    order = sorted(range(1, experts), key=lambda k: -min(k, experts - k))

    for i in range(parts):
        pack(i)
        if i == 0:
            pl.semaphore_wait(barrier, experts + 1)
        for k in order:
            z_copy(i, k).start()
        f_copy(i, 0).start()
    for a, b in zip(here, across):
        a.start()
        b.start()

    def forward(i):
        for k in order:
            z_copy(i, k).wait_recv()
            f_copy(i, k).start()

    hid_step = 256 if ff % 256 == 0 else 128
    side_rows = experts * part

    def compute(i):
        for k in [0] + order:
            f_copy(i, k).wait_recv()
        slots = pl.ds(i * part, part)

        def hidden(j, carry):
            at = pl.ds(pl.multiple_of(j * hid_step, hid_step), hid_step)
            block = rows[i].reshape(2 * side_rows, width)
            grad = lax.dot_general(block, dw[at, :], NT, preferred_element_type=F32)
            for side in range(2):
                for k in range(experts):
                    source = 2 * behind(k) + (1 - h if side else h)
                    low = side * side_rows + k * part
                    piece = grad[low:low + part]
                    g = sg[source, slots, at].astype(F32)
                    u = su[source, slots, at].astype(F32)
                    sigma = 1.0 / (1.0 + jnp.exp(-g))
                    there = pl.ds(low, part)
                    hid_g[there, at] = (piece * u * sigma * (1.0 + g * (1.0 - sigma))).astype(BF16)
                    hid_u[there, at] = (piece * g * sigma).astype(BF16)
            return carry

        lax.fori_loop(0, ff // hid_step, hidden, 0)

        def term(j, carry):
            at = pl.ds(pl.multiple_of(j * chunk, chunk), chunk)
            total = lax.dot_general(hid_g[...], gw[at, :], NT, preferred_element_type=F32)
            total = total + lax.dot_general(hid_u[...], uw[at, :], NT, preferred_element_type=F32)
            total = total.astype(BF16)
            own[i, :, :, at] = total[:side_rows].reshape(experts, part, chunk)
            psend[i, :, :, at] = total[side_rows:].reshape(experts, part, chunk)
            return carry

        lax.fori_loop(0, chunks, term, 0)
        for k in order:
            r_copy(i, k).start()

    def settle(i, k):
        r_copy(i, k).wait_recv()
        f_copy(i, k).wait_send()
        dst = rows.at[i, 0, k] if k else ret.at[i, 0]

        def step(j, carry):
            at = pl.ds(pl.multiple_of(j * chunk, chunk), chunk)
            both = own[i, k, :, at].astype(F32) + precv[i, k, :, at].astype(F32)
            dst[:, at] = both.astype(BF16)
            return carry

        lax.fori_loop(0, chunks, step, 0)
        if k:
            b_copy(i, k).start()

    column = [
        jnp.sum(jnp.where(lane == ahead(k), key, 0.0), axis=1, keepdims=True)
        for k in range(experts)
    ]
    weight = [
        jnp.sum(jnp.where(ids == ahead(k), probs, 0.0), axis=1, keepdims=True)
        for k in range(experts)
    ]
    slot_c = lax.broadcasted_iota(jnp.int32, (tok, part), 1)

    def combine(i, first, last):
        for k in order:
            b_copy(i, k).wait_recv()
        slots = (slot_c + i * part).astype(F32)
        full = jnp.concatenate(
            [jnp.where(column[k] == slots, weight[k], 0.0) for k in range(experts)], axis=1
        )
        terms = []
        for _ in range(3):
            terms.append(full.astype(BF16))
            full = full - terms[-1].astype(F32)

        def step(j, carry):
            at = pl.ds(pl.multiple_of(j * chunk, chunk), chunk)
            block = ret[i, :, :, at].reshape(side_rows, chunk)
            value = sum(jnp.dot(t, block, preferred_element_type=F32) for t in terms)
            if not first:
                value = value + acc[:, at]
            if last:
                out_ref[:, at] = value.astype(BF16)
            else:
                acc[:, at] = value
            return carry

        lax.fori_loop(0, chunks, step, 0)

    for t in range(parts + 2):
        if t < parts:
            forward(t)
        if t == 1:
            for a, b in zip(here, across):
                a.wait()
                b.wait_recv()
        if 0 <= t - 1 < parts:
            compute(t - 1)
        if t - 1 == parts - 1:
            for i in range(parts):
                r_copy(i, 0).start()
        if 0 <= t - 2 < parts:
            for k in order:
                settle(t - 2, k)
    for i in range(parts):
        settle(i, 0)
    for i in range(parts):
        combine(i, i == 0, i == parts - 1)
    for b in across:
        b.wait_send()
    for i in range(parts):
        for k in range(experts):
            r_copy(i, k).wait_send()
            if k:
                z_copy(i, k).wait_send()
                b_copy(i, k).wait_send()


def shards(grad_out, expert_ids, probs, saved_gate, saved_up, gate_weight, up_weight, down_weight):
    n_expert = lax.axis_size("expert")
    experts = n_expert // 2
    tok, width = grad_out.shape
    capacity = saved_gate.shape[3]
    quarter = down_weight.shape[1]
    ff = 2 * quarter
    cap = -(-capacity // 16) * 16
    if cap != capacity:
        pad = ((0, 0), (0, 0), (0, 0), (0, cap - capacity), (0, 0))
        saved_gate = jnp.pad(saved_gate, pad)
        saved_up = jnp.pad(saved_up, pad)
    part = 16
    parts = cap // part
    vmem = pl.BlockSpec(memory_space=pltpu.VMEM)
    hbm = pl.BlockSpec(memory_space=pl.ANY)
    dma = pltpu.SemaphoreType.DMA
    return pl.pallas_call(
        functools.partial(kernel, experts, parts, part),
        out_shape=jax.ShapeDtypeStruct((tok, width), BF16),
        in_specs=[vmem, vmem, vmem, hbm, hbm, hbm, hbm, hbm],
        out_specs=vmem,
        scratch_shapes=[
            pltpu.VMEM((parts, 2, experts, part, width), BF16),
            pltpu.VMEM((parts, experts - 1, part, width), BF16),
            pltpu.VMEM((ff, width), BF16),
            pltpu.VMEM((width, ff), BF16),
            pltpu.VMEM((width, ff), BF16),
            pltpu.VMEM((n_expert, cap, ff), BF16),
            pltpu.VMEM((n_expert, cap, ff), BF16),
            pltpu.VMEM((parts, experts, part, width), BF16),
            pltpu.VMEM((parts, experts, part, width), BF16),
            pltpu.VMEM((parts, experts, part, width), BF16),
            pltpu.VMEM((parts, experts, part, width), BF16),
            pltpu.VMEM((tok, width), F32),
            pltpu.VMEM((tok, 128), F32),
            pltpu.VMEM((2 * experts * part, ff), BF16),
            pltpu.VMEM((2 * experts * part, ff), BF16),
            dma((5,)), dma((5,)), dma((5,)),
            dma((parts, experts)), dma((parts, experts)), dma((parts, experts)), dma((parts, experts)),
            dma((parts, experts)), dma((parts, experts)), dma((parts, experts)), dma((parts, experts)),
        ],
        compiler_params=pltpu.CompilerParams(
            collective_id=0, has_side_effects=True, vmem_limit_bytes=63 * 1024 * 1024
        ),
        cost_estimate=pl.CostEstimate(
            flops=6 * n_expert * cap * ff * width, bytes_accessed=8 * width * ff, transcendentals=0
        ),
    )(grad_out, expert_ids, probs, saved_gate, saved_up, gate_weight, up_weight, down_weight)


def solution(mesh):
    in_specs = (
        P(("group", "expert", "tensor"), None),
        P(("group", "expert", "tensor"), None),
        P(("group", "expert", "tensor"), None),
        P("expert", "group", None, None, "tensor"),
        P("expert", "group", None, None, "tensor"),
        P("expert", None, "tensor"),
        P("expert", None, "tensor"),
        P("expert", "tensor", None),
    )
    out_specs = P(("group", "expert", "tensor"), None)
    return jax.shard_map(shards, mesh=mesh, in_specs=in_specs, out_specs=out_specs, check_vma=False)
```

time: 186 us -> 170 us (0.914)
  Pallas kernels: 180 us -> 165 us
    pallas_call x1, Pallas kernels: 180 us -> 165 us  [shards(): pl.pallas_call(functools.partial(kernel, experts, parts, part), out_shape...]
where the time goes in v2:
time: 170 us
  Pallas kernels  165 us (97%)
  local copies, waits for them, and re-layouts  5.1 us (3%)
    pallas_call x1, Pallas kernels, shards(): pl.pallas_call(functools.partial(kernel, experts, parts, part), out_shape...  165 us
    unnamed x3, local copies, waits for them, and re-layouts  5.1 us

profile of v2, /device:TPU:8, one launch (start us, length us, event | category | flops | bytes accessed | tf_op | source)
XLA Modules:
  0.0 169.9 jit_solution(1378707175344184346)
XLA Ops:
  0.0 1.4 copy.9.ids_ref
  1.4 1.4 copy.10.probs_ref
  2.8 164.8 %shard_map.82 = bf16[128,4096]{1,0:T(8,128)(2,1)} custom-call(bf16[128,4096]{1,0:T(8,128)(2,1)} %go_ref.1, s32[128,2]{1,0:T(8,128)} %copy.9.ids_ref, f32[128,2]{1,0:T(8,128)} %copy.10.probs_ref, bf16[1,8,2,96,384]{4,3,2,1,0:T(8,128)(2,1)} %sg_in.1, bf16[1,8,2,96,384]{4,3,2,1,0:T(8,128)(2,1)} %su_in.1, bf16[1,4096,384]{2,1,0:T(8,128)(2,1)} %gw_in.1, ...), custom_call_target="tpu_custom_call" | custom-call | flops 14495514624 | bytes 25165824 | tf_op jit(solution)/shard_map/pallas_call | solution.py:279
  167.6 2.3 %copy.12 = bf16[128,4096]{1,0:T(8,128)(2,1)} copy(bf16[128,4096]{1,0:T(8,128)(2,1)} %shard_map.82) | data formatting | bytes 2097152
